TPU v7x, 128 devices: a whole 4x4x4 slice. The times are simulated.
128 devices in a mesh: noise: 8 (over y, core), dp: 16 (over x, z).
Axes of the slice: x: 4, y: 4, z: 4, core: 2. Of those that a mesh axis runs over, the one named last changes fastest.
Arguments:
- noise_latents: bfloat16 [16384, 2048], P('noise', 'dp')
- data_latents: bfloat16 [16384, 2048], P('dp', 'noise')
Outputs:
- targets: float32 [16384, 2048], P('noise', 'dp')
- potential_rows: float32 [16384], P('noise')
- potential_cols: float32 [16384], P('dp')
All inputs are finite; a program needn't handle non-finite values.
Results may differ from a plain program's by a relative error of at most 0.0023.
Values may be sent and summed in bfloat16 or wider, within the bound.
A program may use at most 128 MiB of HBM per device.

v0:
```python
import functools
import math

import jax
import jax.numpy as jnp
from jax import lax
from jax.experimental import pallas as pl
from jax.experimental.pallas import tpu as pltpu
from jax.sharding import PartitionSpec as P

ITERS = 3
EPSILON = 0.04
LOG2E = 1.0 / math.log(2.0)
MESH = pl.DeviceIdType.MESH
LANES = 128
TILE = 32
SIDE = 4
PARTS = 4


def spread_lanes(ref, row):
    return jnp.broadcast_to(ref[pl.ds(row, 1), :], (LANES, LANES)).T


def exchange(buf, send, recv, step, me, peers, started):
    for peer in peers:
        pltpu.make_async_remote_copy(
            src_ref=buf.at[step, me],
            dst_ref=buf.at[step, me],
            send_sem=send.at[step],
            recv_sem=recv.at[step],
            device_id=peer,
            device_id_type=MESH,
        ).start()
    slots = buf.at[step, pl.ds(0, len(peers))]
    every = pltpu.make_async_remote_copy(
        src_ref=slots,
        dst_ref=slots,
        send_sem=send.at[step],
        recv_sem=recv.at[step],
        device_id=peers[0],
        device_id_type=MESH,
    )
    every.wait_recv()
    started.append(every)


def combine(buf, step, size):
    top = buf[step, 0]
    for s in range(1, size):
        top = jnp.maximum(top, buf[step, s])
    total = jnp.exp2(buf[step, 0] - top)
    for s in range(1, size):
        total = total + jnp.exp2(buf[step, s] - top)
    return top + jnp.log(total) * LOG2E


def add_slots(buf, step, size):
    total = buf[step, 0]
    for s in range(1, size):
        total = total + buf[step, s]
    return total


def kernel(
    rsize, csize, width,
    noise_ref, data_ref,
    targets, rows_out, cols_out,
    noise_all, data_all, scores, weights,
    shift, first, scale, part, data_part, colvec, rowpack, colpack, sqx, sqy, swap,
    col_buf, row_buf, out_buf, own_buf, far_buf, near_buf, in_sum,
    col_send, col_recv, row_send, row_recv, swap_send, swap_recv,
    cross_send, cross_recv, noise_send, noise_recv, data_send, data_recv,
    sum_send, sum_recv, in_send, in_recv, keep, far_keep, given, give_send, give_recv, part_recv, local_sems, own_send, far_send, relay_in, mate_out, mate_in,
):
    rows, cols = scores.shape
    n = lax.axis_index("noise")
    d = lax.axis_index("dp")
    x, z = d // SIDE, lax.rem(d, SIDE)
    y, core = n // 2, lax.rem(n, 2)
    kind = lax.rem((x + 1) // 2, 2)
    pair = x // 2
    side = lax.rem(x, 2)
    home = core == kind
    kappa = LOG2E / EPSILON
    log_rows = math.log2(rows * csize)
    log_cols = math.log2(cols * rsize)
    chunks = cols // LANES
    row_blocks = rows // LANES
    tiles = rows // TILE
    started = []

    def around(value):
        return lax.rem(value + SIDE, SIDE)

    def device(xi, yi, zi, ci):
        return (yi * 2 + ci, xi * SIDE + zi)

    me_row = pair * SIDE + z
    me_col = y * 4 + kind * 2 + core

    sibling = device(x, y, z, 1 - core)
    partner = x + 1 - 2 * side
    mate = SIDE - 1 - x
    opposite = around(x + 2)

    barrier = pltpu.get_barrier_semaphore()
    ys, zs = [around(y + k) for k in range(SIDE)], [around(z + k) for k in range(SIDE)]
    rings = [yi * 2 + ci for yi in (ys[2], ys[1], ys[3], ys[0]) for ci in (1 - core, core)]
    col_peers = [(r, di) for di in (partner * SIDE + z, d) for r in rings][:-1]
    row_peers = [(n, xi * SIDE + zi) for xi in (mate, x) for zi in (zs[2], zs[1], zs[3], zs[0])][:-1]
    greeted = row_peers + col_peers
    greeted += [device(opposite, y, z, 0), device(opposite, y, z, 1), device(mate, y, z, 1 - core)]
    greeted += [device(x, y, around(z + step), 1 - core) for step in (1, -1)]
    for to in greeted:
        pl.semaphore_signal(barrier, inc=1, device_id=to, device_id_type=MESH)
    pl.semaphore_wait(barrier, len(greeted))

    def remote(src, dst, send, recv, to):
        return pltpu.make_async_remote_copy(
            src_ref=src, dst_ref=dst, send_sem=send, recv_sem=recv, device_id=to, device_id_type=MESH
        )

    def begin(copy):
        copy.start()
        started.append(copy)

    def lane(c):
        return slice(LANES * c, LANES * (c + 1))

    HOP = (1, -1)
    own = x * SIDE + z

    def cross_copy(i, half, to):
        return remote(
            noise_ref.at[pl.ds(half * rows, rows)], noise_all.at[own], cross_send.at[i], cross_recv.at[x], to
        )

    def cross_wait(xi):
        remote(
            noise_ref.at[pl.ds(0, rows)], noise_all.at[xi * SIDE + z], cross_send.at[0], cross_recv.at[xi], sibling
        ).wait_recv()

    there = jnp.where(home, mate, partner)
    aside = cross_copy(2, 1 - core, sibling)

    def noise_copy(xi, t, forward, slot):
        at = pl.ds(t * (rows // 2), rows // 2) if forward else pl.ds(0, rows)
        f = int(forward)
        return remote(
            noise_all.at[slot, at], noise_all.at[slot, at],
            noise_send.at[xi, t, f], noise_recv.at[xi, t, f], device(x, y, around(z + HOP[t]), core),
        )

    def noise_wait(xi, t, forward):
        slot = xi * SIDE + around(z - HOP[t] * (2 if forward else 1))
        noise_copy(xi, t, forward, slot).wait_recv()
        return slot

    def data_copy(r, index, where, lo, size, to, own=False):
        at = pl.ds(lo, size)
        block = side if r == 0 else 1 - side
        dst = data_all.at[block, where, at]
        return remote(data_ref.at[at] if own else dst, dst, data_send.at[r, index], data_recv.at[r, index], to)

    half_cols = cols // 4
    full_cols = cols // 2

    def along_y(step, c):
        return around(y + step) * 2 + c

    def data_wait(r, index, where, lo, size):
        data_copy(r, index, where, lo, size, sibling).wait_recv()

    HALF = 9

    def cross_data(h, own=False):
        at = pl.ds(h * half_cols, half_cols)
        dst = data_all.at[side if own else 1 - side, n, at]
        return remote(
            data_ref.at[at], dst, data_send.at[1, 11 + h], data_recv.at[1, 11 + h], device(partner, y, z, core)
        )

    def partner_y(t, h, back=0):
        where = around(y + back) * 2 + core
        to = device(x, around(y + HOP[t]), z, core)
        return t if h == 0 else HALF + t, where, h * half_cols, half_cols, to

    def partner_wait(t, h):
        data_copy(1, *partner_y(t, h, -HOP[t])).wait_recv()

    def own_round(t, a):
        return remote(
            noise_ref.at[pl.ds(a * rows, rows)], noise_all.at[own],
            own_send.at[t, a], noise_recv.at[x, t, 0], device(x, y, around(z + HOP[t]), a),
        )

    def own_half():
        return pltpu.make_async_copy(
            noise_ref.at[pl.ds(pl.multiple_of(core * rows, rows), rows)], noise_all.at[own], local_sems.at[0]
        )

    @pl.when(home)
    def _():
        for t in (0, 1):
            for a in (0, 1):
                own_round(t, a).start()
        aside.start()

    begin(cross_copy(0, 0, device(there, y, z, 0)))
    begin(cross_copy(1, 1, device(there, y, z, 1)))
    for t in (0, 1):
        begin(data_copy(0, t, n, 0, full_cols, device(x, around(y + HOP[t]), z, core), own=True))
    @pl.when(home)
    def _():
        own_half().start()

    data_own = pltpu.make_async_copy(data_ref, data_all.at[side, n], local_sems.at[1])
    data_own.start()
    scores[...] = jnp.zeros_like(scores)
    part[...] = jnp.zeros_like(part)
    data_part[...] = jnp.zeros_like(data_part)

    def round_z(xi):
        for t in (0, 1):
            begin(noise_copy(xi, t, False, xi * SIDE + z))

    def forward_z(xi):
        for t in (0, 1):
            begin(noise_copy(xi, t, True, noise_wait(xi, t, False)))

    def far_noise(xi, t):
        slot = xi * SIDE + around(z + 2)
        at = pl.ds(t * (rows // 2), rows // 2)
        return remote(
            noise_all.at[slot, at], noise_all.at[slot, at],
            far_send.at[xi, t], noise_recv.at[xi, t, 1], device(mate, y, z, core),
        )

    def share_far(xi):
        for t in (0, 1):
            noise_wait(xi, t, True)
            begin(far_noise(xi, t))

    def far_wait(xi):
        for t in (0, 1):
            far_noise(xi, t).wait_recv()

    def far_data(t, block):
        where = along_y(2, core)
        at = pl.ds(t * half_cols, half_cols)
        dst = data_all.at[block, where, at]
        return remote(dst, dst, data_send.at[1, 2 + t], data_recv.at[1, 2 + t], device(partner, y, z, core))

    cross_wait(partner)
    slot = partner * SIDE + z
    begin(remote(
        noise_all.at[slot], noise_all.at[slot], cross_send.at[3], cross_recv.at[partner], device(mate, y, z, core)
    ))
    round_z(partner)
    for h in (0, 1):
        begin(cross_data(h, own=True))
    begin(data_copy(0, 4, n, 0, full_cols, sibling, own=True))
    forward_z(x)
    cross_wait(mate)
    round_z(mate)
    for t in (0, 1):
        where = along_y(-HOP[t], core)
        data_wait(0, t, where, 0, full_cols)
        begin(data_copy(0, 2 + t, where, t * half_cols, half_cols, device(x, around(y + HOP[t]), z, core)))
        begin(data_copy(0, 5 + t, where, 0, full_cols, sibling))
    cross_data(0).wait_recv()
    for t in (0, 1):
        begin(data_copy(1, *partner_y(t, 0)))
    forward_z(partner)
    cross_wait(opposite)
    round_z(opposite)
    share_far(x)
    cross_data(1).wait_recv()
    for t in (0, 1):
        begin(data_copy(1, *partner_y(t, 1)))
    begin(data_copy(1, 4, n, 0, full_cols, sibling))
    for t in (0, 1):
        where = along_y(2, core)
        data_wait(0, 2 + t, where, t * half_cols, half_cols)
        begin(far_data(t, side))
        begin(data_copy(0, 7 + t, where, t * half_cols, half_cols, sibling))

    def squares(block):
        value = block.astype(jnp.float32)
        return value * value

    def chunk_product(xi, m):
        left = jnp.concatenate([noise_all[xi * SIDE + i] for i in range(SIDE)], axis=1)
        cut = pl.ds(pl.multiple_of(m * 256, 256), 256)
        here = pl.ds(pl.multiple_of(lax.rem(m, 4) * 256, 256), 256)
        pieces = [data_all[m // 4, xi * 2 + i, here, :] for i in (0, 1)]
        total = data_part[cut, :]
        for piece in pieces:
            total = total + squares(piece[:, :LANES]) + squares(piece[:, LANES:])
        data_part[cut, :] = total
        return lax.dot_general(
            left, jnp.concatenate(pieces, axis=1), (((1,), (1,)), ((), ())), preferred_element_type=jnp.float32
        )

    def norms(xi):
        def norm(r, carry):
            cut = pl.ds(pl.multiple_of(r * 64, 64), 64)
            total = part[cut, :]
            for i in range(SIDE):
                total = total + squares(noise_all[xi * SIDE + i, cut, :])
            part[cut, :] = total
            return carry

        lax.fori_loop(0, rows // 64, norm, 0)

    near, other_block = side * 4, 4 - side * 4

    def unit(block, xs, fresh, count=4):
        def column(i, carry):
            m = block + i
            cut = pl.ds(pl.multiple_of(m * 256, 256), 256)
            value = None if fresh else scores[:, cut]
            for xi in xs:
                value = chunk_product(xi, m) if value is None else value + chunk_product(xi, m)
            scores[:, cut] = value
            return carry

        lax.fori_loop(0, count, column, 0)

    def add_unit(block, count, xi):
        unit(block, (xi,), False, count)

    data_own.wait()
    data_wait(0, 4, along_y(0, 1 - core), 0, full_cols)
    for t in (0, 1):
        data_wait(0, 5 + t, along_y(-HOP[t], 1 - core), 0, full_cols)
    for t in (0, 1):
        data_wait(0, 7 + t, along_y(2, 1 - core), t * half_cols, half_cols)

    @pl.when(home)
    def _():
        own_half().wait()

    @pl.when(jnp.logical_not(home))
    def _():
        cross_wait(x)

    unit(near, (x,), True)
    share_far(partner)
    norms(x)
    for t in (0, 1):
        noise_wait(mate, t, False)
    far_wait(mate)
    unit(near, (mate,), False)
    norms(mate)

    def beside(t, h, c):
        return data_copy(1, (5 if h == 0 else 13) + t, along_y(-HOP[t], c), h * half_cols, half_cols, sibling)

    for t in (0, 1):
        partner_wait(t, 0)
        begin(beside(t, 0, core))
    unit(near, (partner,), False)
    norms(partner)
    data_wait(1, 4, along_y(0, 1 - core), 0, full_cols)
    for t in (0, 1):
        beside(t, 0, 1 - core).wait_recv()

    def ahead(i, carry):
        xi = around(y + i + i // 2)
        add_unit(other_block, jnp.where(xi == opposite, 0, jnp.where(i == 0, 4, 2)), xi)
        return carry

    lax.fori_loop(0, 3, ahead, 0)
    for t in (0, 1):
        partner_wait(t, 1)
        begin(beside(t, 1, core))
    for t in (0, 1):
        noise_wait(opposite, t, False)
    far_wait(opposite)
    for t in (0, 1):
        far_data(t, 1 - side).wait_recv()
        begin(data_copy(1, 7 + t, along_y(2, core), t * half_cols, half_cols, sibling))
    norms(opposite)

    factor = 2.0 * kappa / width

    def row_shift(r, carry):
        at = pl.ds(pl.multiple_of(r * 128, 128), 128)
        total = jnp.sum(part[at, :], axis=1, keepdims=True) * (-kappa / width)
        shift[at, :] = jnp.broadcast_to(total, (128, LANES))
        return carry

    lax.fori_loop(0, rows // 128, row_shift, 0)

    def final(block, xi):
        def column(i, carry):
            m = block + i
            cut = pl.ds(pl.multiple_of(m * 256, 256), 256)
            value = (scores[:, cut] + chunk_product(xi, m)) * factor
            scores[:, cut] = value
            for e in (0, 1):
                top = jnp.max(value[:, LANES * e:LANES * (e + 1)] + shift[...], axis=0, keepdims=True)
                colvec[:, pl.ds(pl.multiple_of(m * 256 + e * LANES, LANES), LANES)] = jnp.broadcast_to(top, (8, LANES))
            return carry

        lax.fori_loop(0, 4, column, 0)

    final(near, opposite)
    add_unit(other_block, jnp.where(opposite == y, 4, jnp.where(opposite == around(y + 2), 0, 2)), opposite)
    for t in (0, 1):
        beside(t, 1, 1 - core).wait_recv()
    unit(other_block + 2, (around(y + 1), around(y - 1)), False, 2)
    for t in (0, 1):
        data_wait(1, 7 + t, along_y(2, 1 - core), t * half_cols, half_cols)
    final(other_block, around(y + 2))

    def fold(block, op):
        out = block[0:8]
        for r in range(1, TILE // 8):
            out = op(out, block[8 * r:8 * r + 8])
        return out

    def spread_cols():
        for c in range(chunks):
            colvec[:, lane(c)] = jnp.broadcast_to(colpack[pl.ds(c, 1), :], (8, LANES))

    def tall(ref, c):
        return jnp.concatenate([ref[:, lane(c)]] * (TILE // 8), axis=0)

    def tile_at(t):
        return pl.ds(pl.multiple_of(t * TILE, TILE), TILE)

    def loop(body, init):
        return lax.fori_loop(0, tiles, body, init, unroll=2)

    zeros = tuple(jnp.zeros((8, LANES), jnp.float32) for _ in range(chunks))

    def exp_step(t, accs):
        at = tile_at(t)
        add = shift[at, :]
        return tuple(
            accs[c] + fold(jnp.exp2(scores[at, lane(c)] + add - tall(colvec, c)), jnp.add)
            for c in range(chunks)
        )

    sums = loop(exp_step, zeros)
    for c in range(chunks):
        total = jnp.sum(sums[c], axis=0, keepdims=True)
        col_buf[0, me_col, pl.ds(c, 1), :] = colvec[0:1, lane(c)] + jnp.log(total) * LOG2E
    exchange(col_buf, col_send, col_recv, 0, me_col, col_peers, started)
    col_pot = -log_cols - combine(col_buf, 0, csize)
    colpack[...] = col_pot
    spread_cols()

    def row_step(t, carry):
        at = tile_at(t)
        top = scores[at, lane(0)] + tall(colvec, 0)
        for c in range(1, chunks):
            top = jnp.maximum(top, scores[at, lane(c)] + tall(colvec, c))
        first[at, :] = top
        total = None
        for c in range(chunks):
            value = jnp.exp2(scores[at, lane(c)] + tall(colvec, c) - top)
            scores[at, lane(c)] = value
            total = value if total is None else total + value
        part[at, :] = total
        return carry

    loop(row_step, 0)
    for b in range(row_blocks):
        at = pl.ds(b * LANES, LANES)
        tops = first[at, :].T
        top = jnp.max(tops, axis=0, keepdims=True)
        total = jnp.sum(part[at, :].T * jnp.exp2(tops - top), axis=0, keepdims=True)
        row_buf[0, me_row, pl.ds(b, 1), :] = top + jnp.log(total) * LOG2E
    exchange(row_buf, row_send, row_recv, 0, me_row, row_peers, started)
    row_lse = combine(row_buf, 0, rsize)
    rowpack[...] = row_lse
    for b in range(row_blocks):
        at = pl.ds(b * LANES, LANES)
        base = jnp.exp2(first[at, :] - spread_lanes(rowpack, b))
        first[at, :] = base
        scale[at, :] = base

    def col_step(t, accs):
        at = tile_at(t)
        mul = scale[at, :]
        return tuple(accs[c] + fold(scores[at, lane(c)] * mul, jnp.add) for c in range(chunks))

    def sum_step(keep_values):
        def body(t, carry):
            at = tile_at(t)
            total = None
            for c in range(chunks):
                value = scores[at, lane(c)] * tall(colvec, c)
                if keep_values:
                    scores[at, lane(c)] = value
                total = value if total is None else total + value
            part[at, :] = total * first[at, :]
            return carry

        return body

    for step in range(1, ITERS):
        sums = loop(col_step, zeros)
        for c in range(chunks):
            col_buf[step, me_col, pl.ds(c, 1), :] = jnp.sum(sums[c], axis=0, keepdims=True)
        exchange(col_buf, col_send, col_recv, step, me_col, col_peers, started)
        ratio = 1.0 / add_slots(col_buf, step, csize)
        colpack[...] = ratio
        spread_cols()
        loop(sum_step(step == ITERS - 1), 0)
        for b in range(row_blocks):
            at = pl.ds(b * LANES, LANES)
            row_buf[step, me_row, pl.ds(b, 1), :] = jnp.sum(part[at, :].T, axis=0, keepdims=True)
        exchange(row_buf, row_send, row_recv, step, me_row, row_peers, started)
        total = add_slots(row_buf, step, rsize)
        rowpack[...] = 1.0 / total
        for b in range(row_blocks):
            at = pl.ds(b * LANES, LANES)
            scale[at, :] = first[at, :] * spread_lanes(rowpack, b)

    def weigh(r):
        def body(t, carry):
            at = pl.ds(pl.multiple_of(r * (rows // 2) + t * TILE, TILE), TILE)
            mul = scale[at, :]
            for c in range(chunks):
                weights[at, lane(c)] = (scores[at, lane(c)] * mul).astype(jnp.bfloat16)
            return carry

        lax.fori_loop(0, tiles // 2, body, 0, unroll=2)

    def swap_copy(i, to):
        return remote(swap.at[0], swap.at[i], swap_send.at[i], swap_recv.at[i], to)

    def potentials():
        for c in range(chunks):
            sqy[pl.ds(c, 1), :] = jnp.sum(data_part[pl.ds(c * LANES, LANES), :].T, axis=0, keepdims=True)
        cols_pot = (col_pot + jnp.log(ratio) * LOG2E + (log_rows - log_cols)) / kappa + sqy[...] / width
        colpack[...] = cols_pot
        cols_out[...] = colpack[pl.ds(pl.multiple_of(side * 8, 8), 8), :]
        for b in range(row_blocks):
            sqx[pl.ds(b, 1), :] = shift[pl.ds(b * LANES, LANES), :].T[0:1]
        swap[0] = -(log_rows + row_lse + jnp.log(total) * LOG2E + sqx[...]) / kappa
        begin(swap_copy(1, sibling))
        for i in (0, 1):
            begin(remote(
                swap.at[0], swap.at[2 + core], swap_send.at[2 + i], swap_recv.at[2 + core], device(partner, y, z, i)
            ))

    strip = rows // 2

    def half_rows(r):
        return pl.ds(pl.multiple_of(r * strip, strip), strip)

    def block_x(b):
        return jnp.where(b < 2, jnp.where(b == 0, opposite, mate), jnp.where(b == 2, partner, x))

    def product(p, r, to_z):
        cut = pl.ds(pl.multiple_of(lax.rem(to_z, 2) * LANES, LANES), LANES)
        total = None
        for k in (0, 1):
            block = jnp.concatenate(
                [data_all[k, block_x(2 * p + e) * 2 + to_z // 2, :, cut] for e in (0, 1)], axis=1
            )
            value = jnp.dot(
                weights[half_rows(r), k * full_cols:(k + 1) * full_cols], block,
                preferred_element_type=jnp.float32,
            )
            total = value if total is None else total + value
        return total

    def hop(t):
        return 1 - 2 * t

    def sum_copy(b, t, index, src, dst):
        to = device(x, y, around(z + hop(t)), core)
        return remote(src, dst, sum_send.at[b, t, index], sum_recv.at[b, t, index], to)

    def far_copy(b, t):
        return sum_copy(b, t, 0, out_buf.at[b, 2, half_rows(t)], far_buf.at[b - 2, t])

    def direct_copy(b, t):
        at = half_rows(1 - t)
        return sum_copy(b, t, 1, out_buf.at[b, t, at], near_buf.at[b, t, at])

    def added_copy(b, t):
        at = half_rows(t)
        return sum_copy(b, t, 2, out_buf.at[b, t, at], near_buf.at[b, t, at])

    def give_copy(b, r):
        at = half_rows(r)
        return remote(
            out_buf.at[b, 2, at], given.at[b, at], give_send.at[b, r], give_recv.at[b, r], device(mate, y, z, core)
        )

    def relay_copy(r):
        at = half_rows(r)
        return remote(own_buf.at[0, at], relay_in.at[at], in_send.at[r], in_recv.at[4 + r], device(mate, y, z, core))

    def partner_copy(a, r):
        at = half_rows(r)
        return remote(
            own_buf.at[2, at], in_sum.at[a, at], in_send.at[2 + r], part_recv.at[a, r], device(partner, y, z, kind)
        )

    def mate_copy(a):
        return remote(mate_out, mate_in.at[a], in_send.at[4], in_recv.at[2 + a], device(mate, y, z, kind))

    def stay_copy(a):
        return remote(own_buf.at[3], in_sum.at[a], in_send.at[5], in_recv.at[a], sibling)

    def add_far(b):
        for t in (0, 1):
            far_copy(b, t).wait_recv()
            out_buf[b, t, half_rows(t), :] = (
                keep[b - 2, t, half_rows(t), :] + far_buf[b - 2, t].astype(jnp.float32)
            ).astype(jnp.bfloat16)
            added_copy(b, t).start()

    def add_near(b):
        for t in (0, 1):
            direct_copy(b, t).wait_recv()
            added_copy(b, t).wait_recv()
        own_buf[b] = own_buf[b] + near_buf[b, 0].astype(jnp.float32) + near_buf[b, 1].astype(jnp.float32)

    def add_given(b):
        for r in (0, 1):
            at = half_rows(r)
            give_copy(b - 2, r).wait_recv()
            out_buf[b, 2, at, :] = (far_keep[b - 2, at, :] + given[b - 2, at, :].astype(jnp.float32)).astype(jnp.bfloat16)
            far_copy(b, r).start()

    def halves(body):
        def step(r, carry):
            body(r)
            return carry

        lax.fori_loop(0, 2, step, 0)

    def give(r):
        weigh(r)
        value = product(0, r, around(z + 2))
        for e in (0, 1):
            out_buf[e, 2, half_rows(r), :] = value[:, lane(e)].astype(jnp.bfloat16)
        give_copy(0, r).start()

    def near_products(p):
        def along(t):
            def part_of(r):
                value = product(p, r, around(z + hop(t)))
                for e in (0, 1):
                    block = value[:, lane(e)]
                    out_buf[2 * p + e, t, half_rows(r), :] = block.astype(jnp.bfloat16)
                    if p == 1:
                        keep[e, t, half_rows(r), :] = block

            halves(part_of)
            direct_copy(2 * p, t).start()
            if p == 0:
                added_copy(0, t).start()

        halves(along)

    def far_products(r):
        value = product(1, r, around(z + 2))
        for e in (0, 1):
            far_keep[e, half_rows(r), :] = value[:, lane(e)]

    def own_products(p):
        def part_of(r):
            value = product(p, r, z)
            for e in (0, 1):
                own_buf[2 * p + e, half_rows(r), :] = value[:, lane(e)]

        halves(part_of)

    halves(give)
    for r in (0, 1):
        give_copy(1, r).start()
    near_products(1)
    near_products(0)
    halves(far_products)
    add_given(2)
    for t in (0, 1):
        direct_copy(1, t).start()
        added_copy(1, t).start()
    halves(own_products)
    add_near(0)
    for r in (0, 1):
        relay_copy(r).start()
    add_far(2)
    add_given(3)
    for t in (0, 1):
        direct_copy(3, t).start()
    add_near(1)
    mate_out[...] = own_buf[1].astype(jnp.bfloat16)
    mate_copy(core).start()
    potentials()
    add_near(2)

    def to_partner(r):
        relay_copy(r).wait_recv()
        own_buf[2, half_rows(r), :] = own_buf[2, half_rows(r), :] + relay_in[half_rows(r), :]
        partner_copy(core, r).start()

    to_partner(0)
    add_far(3)
    to_partner(1)

    swap_copy(1, sibling).wait_recv()
    for i in (0, 1):
        remote(swap.at[0], swap.at[2 + i], swap_send.at[2 + i], swap_recv.at[2 + i], sibling).wait_recv()
    half = rows // LANES
    for a in (0, 1):
        mine_row = jnp.where(core == a, swap[0], swap[1])
        rows_out[pl.ds(a * half, half), :] = jnp.where(home, mine_row, swap[2 + a])

    add_near(3)

    @pl.when(home)
    def _():
        in_sum[core] = own_buf[3]
        stay_copy(1 - core).wait_recv()
        for a in (0, 1):
            mate_copy(a).wait_recv()
            in_sum[a] = in_sum[a] + mate_in[a].astype(jnp.float32)

    @pl.when(jnp.logical_not(home))
    def _():
        stay_copy(core).start()
        for a in (0, 1):
            for r in (0, 1):
                partner_copy(a, r).wait_recv()

    def result_copy(a):
        return pltpu.make_async_copy(in_sum.at[a], targets.at[pl.ds(a * rows, rows)], local_sems.at[a])

    for a in (0, 1):
        result_copy(a).start()

    def settle(b, carry):
        for t in (0, 1):
            direct_copy(b, t).wait_send()
            added_copy(b, t).wait_send()

            @pl.when(b < 2)
            def _():
                give_copy(jnp.minimum(b, 1), t).wait_send()

            @pl.when(b >= 2)
            def _():
                far_copy(jnp.maximum(b, 2), t).wait_send()

        return carry

    lax.fori_loop(0, SIDE, settle, 0)
    for a in (0, 1):
        result_copy(a).wait()
    for r in (0, 1):
        relay_copy(r).wait_send()
        partner_copy(core, r).wait_send()
    mate_copy(core).wait_send()

    @pl.when(jnp.logical_not(home))
    def _():
        stay_copy(core).wait_send()

    for copy in started:
        copy.wait_send()

    @pl.when(home)
    def _():
        aside.wait_send()
        for t in (0, 1):
            for a in (0, 1):
                own_round(t, a).wait_send()


def hand_on(targets, rows_pot, cols_pot, targets_out, rows_out, cols_out, stage, row_stage, col_stage, sems):
    size = targets.shape[0] // PARTS
    legs = [
        (targets.at[pl.ds(i * size, size)], stage.at[i], targets_out.at[pl.ds(i * size, size)]) for i in range(PARTS)
    ]
    legs += [(rows_pot, row_stage, rows_out), (cols_pot, col_stage, cols_out)]
    first = [pltpu.make_async_copy(src, mid, sems.at[i, 0]) for i, (src, mid, _) in enumerate(legs)]
    second = [pltpu.make_async_copy(mid, dst, sems.at[i, 1]) for i, (_, mid, dst) in enumerate(legs)]
    for copy in first:
        copy.start()
    for before, copy in zip(first, second):
        before.wait()
        copy.start()
    for copy in second:
        copy.wait()


def shards(noise_latents, data_latents):
    nsize = lax.axis_size("noise")
    dsize = lax.axis_size("dp")
    block, piece = noise_latents.shape
    rows, cols = block // 2, 2 * data_latents.shape[0]
    rsize, csize = dsize // 2, nsize * 2
    vmem = pl.BlockSpec(memory_space=pltpu.VMEM)
    f32, bf16 = jnp.float32, jnp.bfloat16
    strip = rows // 2
    row_vec, col_vec = (rows // LANES, LANES), (cols // LANES, LANES)
    sems = pltpu.SemaphoreType.DMA
    targets, rows_pot, cols_pot = pl.pallas_call(
        functools.partial(kernel, rsize, csize, piece * dsize),
        out_shape=(
            jax.ShapeDtypeStruct((block, piece), f32),
            jax.ShapeDtypeStruct((block // LANES, LANES), f32),
            jax.ShapeDtypeStruct((cols // 2 // LANES, LANES), f32),
        ),
        in_specs=[pl.BlockSpec(memory_space=pl.ANY)] * 2,
        out_specs=(pl.BlockSpec(memory_space=pl.ANY), vmem, vmem),
        scratch_shapes=[
            pltpu.VMEM((dsize, rows, piece), bf16),
            pltpu.VMEM((2, nsize) + data_latents.shape, bf16),
            pltpu.VMEM((rows, cols), f32),
            pltpu.VMEM((rows, cols), bf16),
            pltpu.VMEM((rows, LANES), f32),
            pltpu.VMEM((rows, LANES), f32),
            pltpu.VMEM((rows, LANES), f32),
            pltpu.VMEM((rows, LANES), f32),
            pltpu.VMEM((cols, LANES), f32),
            pltpu.VMEM((8, cols), f32),
            pltpu.VMEM(row_vec, f32),
            pltpu.VMEM(col_vec, f32),
            pltpu.VMEM(row_vec, f32),
            pltpu.VMEM(col_vec, f32),
            pltpu.VMEM((4,) + row_vec, f32),
            pltpu.VMEM((ITERS, csize) + col_vec, f32),
            pltpu.VMEM((ITERS, rsize) + row_vec, f32),
            pltpu.VMEM((SIDE, 3, rows, LANES), bf16),
            pltpu.VMEM((SIDE, rows, LANES), f32),
            pltpu.VMEM((2, 2, strip, LANES), bf16),
            pltpu.VMEM((SIDE, 2, rows, LANES), bf16),
            pltpu.VMEM((2, rows, LANES), f32),
            sems((ITERS,)),
            sems((ITERS,)),
            sems((ITERS,)),
            sems((ITERS,)),
            sems((4,)),
            sems((4,)),
            sems((4,)),
            sems((4,)),
            sems((SIDE, 2, 2)),
            sems((SIDE, 2, 2)),
            sems((2, 15)),
            sems((2, 15)),
            sems((SIDE, 2, 3)),
            sems((SIDE, 2, 3)),
            sems((6,)),
            sems((6,)),
            pltpu.VMEM((2, 2, rows, LANES), f32),
            pltpu.VMEM((2, rows, LANES), f32),
            pltpu.VMEM((2, rows, LANES), bf16),
            sems((2, 2)),
            sems((2, 2)),
            sems((2, 2)),
            sems((2,)),
            sems((2, 2)),
            sems((SIDE, 2)),
            pltpu.VMEM((rows, LANES), f32),
            pltpu.VMEM((rows, LANES), bf16),
            pltpu.VMEM((2, rows, LANES), bf16),
        ],
        compiler_params=pltpu.CompilerParams(
            collective_id=0, has_side_effects=True, vmem_limit_bytes=60 * 2**20
        ),
    )(noise_latents, data_latents)
    results = (targets, rows_pot, cols_pot)
    targets, rows_pot, cols_pot = pl.pallas_call(
        hand_on,
        out_shape=tuple(jax.ShapeDtypeStruct(a.shape, a.dtype) for a in results),
        in_specs=[pl.BlockSpec(memory_space=pl.ANY)] * 3,
        out_specs=(pl.BlockSpec(memory_space=pl.ANY),) * 3,
        scratch_shapes=[
            pltpu.VMEM((PARTS, block // PARTS, piece), f32),
            pltpu.VMEM(rows_pot.shape, f32),
            pltpu.VMEM(cols_pot.shape, f32),
            sems((PARTS + 2, 2)),
        ],
        compiler_params=pltpu.CompilerParams(vmem_limit_bytes=60 * 2**20),
    )(*results)
    return targets, rows_pot.reshape(block), cols_pot.reshape(cols // 2)


def solution(mesh):
    return jax.shard_map(
        shards,
        mesh=mesh,
        in_specs=(P("noise", "dp"), P("dp", "noise")),
        out_specs=(P("noise", "dp"), P("noise"), P("dp")),
        check_vma=False,
    )
```

profile of v0, /device:TPU:1, one launch (start us, length us, event | category | flops | bytes accessed | tf_op | source)
XLA Modules:
  0.0 126.5 jit_solution(15181104972463900436)
XLA Ops:
  0.6 123.8 %shard_map.49 = (f32[2048,128]{1,0:T(8,128)}, f32[16,128]{1,0:T(8,128)}, f32[8,128]{1,0:T(8,128)}) custom-call(bf16[2048,128]{1,0:T(8,128)(2,1)} %noise_ref.1, bf16[1024,256]{1,0:T(8,128)(2,1)} %data_ref.1), custom_call_target="tpu_custom_call" | custom-call | tf_op jit(solution)/shard_map/pallas_call | solution.py:810
  124.4 2.0 %shard_map.50 = (f32[2048,128]{1,0:T(8,128)}, f32[16,128]{1,0:T(8,128)}, f32[8,128]{1,0:T(8,128)}) custom-call(f32[2048,128]{1,0:T(8,128)} %get-tuple-element.9.targets, f32[16,128]{1,0:T(8,128)} %get-tuple-element.10.rows_pot, f32[8,128]{1,0:T(8,128)} %get-tuple-element.11.cols_pot), custom_call_target="tpu_custom_call" | custom-call | tf_op jit(solution)/shard_map/pallas_call | solution.py:876
where the time goes:
time: 127 us; the launch traced here: 126 us
  Pallas kernels  126 us (99%)
    pallas_call x1, Pallas kernels, shards(): pl.pallas_call(functools.partial(kernel, rsize, csize, piece * dsize), ou...  124 us

commit v1 on v0

--- a/solution.py
+++ b/solution.py
@@ -129,38 +129,46 @@
         return slice(LANES * c, LANES * (c + 1))
 
     HOP = (1, -1)
-    own = x * SIDE + z
+
+    def noise_slot(xi, zi, at):
+        return noise_all.at[xi, at, pl.ds(pl.multiple_of(zi * LANES, LANES), LANES)]
+
+    own = noise_slot(x, z, pl.ds(0, rows))
 
     def cross_copy(i, half, to):
         return remote(
-            noise_ref.at[pl.ds(half * rows, rows)], noise_all.at[own], cross_send.at[i], cross_recv.at[x], to
+            noise_ref.at[pl.ds(half * rows, rows)], own, cross_send.at[i], cross_recv.at[x], to
         )
 
     def cross_wait(xi):
         remote(
-            noise_ref.at[pl.ds(0, rows)], noise_all.at[xi * SIDE + z], cross_send.at[0], cross_recv.at[xi], sibling
+            noise_ref.at[pl.ds(0, rows)], noise_slot(xi, z, pl.ds(0, rows)), cross_send.at[0], cross_recv.at[xi], sibling
         ).wait_recv()
 
     there = jnp.where(home, mate, partner)
     aside = cross_copy(2, 1 - core, sibling)
 
-    def noise_copy(xi, t, forward, slot):
+    def noise_copy(xi, t, forward, zi):
         at = pl.ds(t * (rows // 2), rows // 2) if forward else pl.ds(0, rows)
         f = int(forward)
+        slot = noise_slot(xi, zi, at)
         return remote(
-            noise_all.at[slot, at], noise_all.at[slot, at],
-            noise_send.at[xi, t, f], noise_recv.at[xi, t, f], device(x, y, around(z + HOP[t]), core),
+            slot, slot, noise_send.at[xi, t, f], noise_recv.at[xi, t, f], device(x, y, around(z + HOP[t]), core)
         )
 
     def noise_wait(xi, t, forward):
-        slot = xi * SIDE + around(z - HOP[t] * (2 if forward else 1))
-        noise_copy(xi, t, forward, slot).wait_recv()
-        return slot
+        zi = around(z - HOP[t] * (2 if forward else 1))
+        noise_copy(xi, t, forward, zi).wait_recv()
+        return zi
+
+    def data_slot(block, where, at):
+        width_at = pl.ds(pl.multiple_of(lax.rem(where, 2) * 256, 256), 256)
+        return data_all.at[block, where // 2, at, width_at]
 
     def data_copy(r, index, where, lo, size, to, own=False):
         at = pl.ds(lo, size)
         block = side if r == 0 else 1 - side
-        dst = data_all.at[block, where, at]
+        dst = data_slot(block, where, at)
         return remote(data_ref.at[at] if own else dst, dst, data_send.at[r, index], data_recv.at[r, index], to)
 
     half_cols = cols // 4
@@ -176,7 +184,7 @@
 
     def cross_data(h, own=False):
         at = pl.ds(h * half_cols, half_cols)
-        dst = data_all.at[side if own else 1 - side, n, at]
+        dst = data_slot(side if own else 1 - side, n, at)
         return remote(
             data_ref.at[at], dst, data_send.at[1, 11 + h], data_recv.at[1, 11 + h], device(partner, y, z, core)
         )
@@ -191,13 +199,13 @@
 
     def own_round(t, a):
         return remote(
-            noise_ref.at[pl.ds(a * rows, rows)], noise_all.at[own],
+            noise_ref.at[pl.ds(a * rows, rows)], own,
             own_send.at[t, a], noise_recv.at[x, t, 0], device(x, y, around(z + HOP[t]), a),
         )
 
     def own_half():
         return pltpu.make_async_copy(
-            noise_ref.at[pl.ds(pl.multiple_of(core * rows, rows), rows)], noise_all.at[own], local_sems.at[0]
+            noise_ref.at[pl.ds(pl.multiple_of(core * rows, rows), rows)], own, local_sems.at[0]
         )
 
     @pl.when(home)
@@ -215,7 +223,7 @@
     def _():
         own_half().start()
 
-    data_own = pltpu.make_async_copy(data_ref, data_all.at[side, n], local_sems.at[1])
+    data_own = pltpu.make_async_copy(data_ref, data_slot(side, n, pl.ds(0, full_cols)), local_sems.at[1])
     data_own.start()
     scores[...] = jnp.zeros_like(scores)
     part[...] = jnp.zeros_like(part)
@@ -223,19 +231,15 @@
 
     def round_z(xi):
         for t in (0, 1):
-            begin(noise_copy(xi, t, False, xi * SIDE + z))
+            begin(noise_copy(xi, t, False, z))
 
     def forward_z(xi):
         for t in (0, 1):
             begin(noise_copy(xi, t, True, noise_wait(xi, t, False)))
 
     def far_noise(xi, t):
-        slot = xi * SIDE + around(z + 2)
-        at = pl.ds(t * (rows // 2), rows // 2)
-        return remote(
-            noise_all.at[slot, at], noise_all.at[slot, at],
-            far_send.at[xi, t], noise_recv.at[xi, t, 1], device(mate, y, z, core),
-        )
+        slot = noise_slot(xi, around(z + 2), pl.ds(t * (rows // 2), rows // 2))
+        return remote(slot, slot, far_send.at[xi, t], noise_recv.at[xi, t, 1], device(mate, y, z, core))
 
     def share_far(xi):
         for t in (0, 1):
@@ -249,14 +253,12 @@
     def far_data(t, block):
         where = along_y(2, core)
         at = pl.ds(t * half_cols, half_cols)
-        dst = data_all.at[block, where, at]
+        dst = data_slot(block, where, at)
         return remote(dst, dst, data_send.at[1, 2 + t], data_recv.at[1, 2 + t], device(partner, y, z, core))
 
     cross_wait(partner)
-    slot = partner * SIDE + z
-    begin(remote(
-        noise_all.at[slot], noise_all.at[slot], cross_send.at[3], cross_recv.at[partner], device(mate, y, z, core)
-    ))
+    slot = noise_slot(partner, z, pl.ds(0, rows))
+    begin(remote(slot, slot, cross_send.at[3], cross_recv.at[partner], device(mate, y, z, core)))
     round_z(partner)
     for h in (0, 1):
         begin(cross_data(h, own=True))
@@ -291,16 +293,15 @@
         return value * value
 
     def chunk_product(xi, m):
-        left = jnp.concatenate([noise_all[xi * SIDE + i] for i in range(SIDE)], axis=1)
         cut = pl.ds(pl.multiple_of(m * 256, 256), 256)
         here = pl.ds(pl.multiple_of(lax.rem(m, 4) * 256, 256), 256)
-        pieces = [data_all[m // 4, xi * 2 + i, here, :] for i in (0, 1)]
         total = data_part[cut, :]
-        for piece in pieces:
-            total = total + squares(piece[:, :LANES]) + squares(piece[:, LANES:])
+        for i in range(SIDE):
+            total = total + squares(data_all[m // 4, xi, here, lane(i)])
         data_part[cut, :] = total
         return lax.dot_general(
-            left, jnp.concatenate(pieces, axis=1), (((1,), (1,)), ((), ())), preferred_element_type=jnp.float32
+            noise_all[xi], data_all[m // 4, xi, here, :], (((1,), (1,)), ((), ())),
+            preferred_element_type=jnp.float32,
         )
 
     def norms(xi):
@@ -308,7 +309,7 @@
             cut = pl.ds(pl.multiple_of(r * 64, 64), 64)
             total = part[cut, :]
             for i in range(SIDE):
-                total = total + squares(noise_all[xi * SIDE + i, cut, :])
+                total = total + squares(noise_all[xi, cut, lane(i)])
             part[cut, :] = total
             return carry
 
@@ -559,11 +560,11 @@
         return jnp.where(b < 2, jnp.where(b == 0, opposite, mate), jnp.where(b == 2, partner, x))
 
     def product(p, r, to_z):
-        cut = pl.ds(pl.multiple_of(lax.rem(to_z, 2) * LANES, LANES), LANES)
+        cut = pl.ds(pl.multiple_of(to_z * LANES, LANES), LANES)
         total = None
         for k in (0, 1):
             block = jnp.concatenate(
-                [data_all[k, block_x(2 * p + e) * 2 + to_z // 2, :, cut] for e in (0, 1)], axis=1
+                [data_all[k, block_x(2 * p + e), :, cut] for e in (0, 1)], axis=1
             )
             value = jnp.dot(
                 weights[half_rows(r), k * full_cols:(k + 1) * full_cols], block,
@@ -817,8 +818,8 @@
         in_specs=[pl.BlockSpec(memory_space=pl.ANY)] * 2,
         out_specs=(pl.BlockSpec(memory_space=pl.ANY), vmem, vmem),
         scratch_shapes=[
-            pltpu.VMEM((dsize, rows, piece), bf16),
-            pltpu.VMEM((2, nsize) + data_latents.shape, bf16),
+            pltpu.VMEM((SIDE, rows, SIDE * piece), bf16),
+            pltpu.VMEM((2, SIDE, cols // 2, nsize // SIDE * data_latents.shape[1]), bf16),
             pltpu.VMEM((rows, cols), f32),
             pltpu.VMEM((rows, cols), bf16),
             pltpu.VMEM((rows, LANES), f32),

time: 127 us -> 127 us (level)
  no operation moved by 1% of the time
where the time goes in v1:
time: 127 us
  Pallas kernels  126 us (99%)
    pallas_call x1, Pallas kernels, shards(): pl.pallas_call(functools.partial(kernel, rsize, csize, piece * dsize), ou...  124 us

profile of v1, /device:TPU:1, one launch (start us, length us, event | category | flops | bytes accessed | tf_op | source)
XLA Modules:
  0.0 126.9 jit_solution(14639615991241566547)
XLA Ops:
  0.6 124.2 %shard_map.49 = (f32[2048,128]{1,0:T(8,128)}, f32[16,128]{1,0:T(8,128)}, f32[8,128]{1,0:T(8,128)}) custom-call(bf16[2048,128]{1,0:T(8,128)(2,1)} %noise_ref.1, bf16[1024,256]{1,0:T(8,128)(2,1)} %data_ref.1), custom_call_target="tpu_custom_call" | custom-call | tf_op jit(solution)/shard_map/pallas_call | solution.py:811
  124.9 2.0 %shard_map.50 = (f32[2048,128]{1,0:T(8,128)}, f32[16,128]{1,0:T(8,128)}, f32[8,128]{1,0:T(8,128)}) custom-call(f32[2048,128]{1,0:T(8,128)} %get-tuple-element.9.targets, f32[16,128]{1,0:T(8,128)} %get-tuple-element.10.rows_pot, f32[8,128]{1,0:T(8,128)} %get-tuple-element.11.cols_pot), custom_call_target="tpu_custom_call" | custom-call | tf_op jit(solution)/shard_map/pallas_call | solution.py:877

commit v2 on v1

--- a/solution.py
+++ b/solution.py
@@ -67,7 +67,7 @@
     noise_ref, data_ref,
     targets, rows_out, cols_out,
     noise_all, data_all, scores, weights,
-    shift, first, scale, part, data_part, colvec, rowpack, colpack, sqx, sqy, swap,
+    shift, first, factor_of, scale, part, data_part, colvec, rowpack, colpack, sqx, sqy, swap,
     col_buf, row_buf, out_buf, own_buf, far_buf, near_buf, in_sum,
     col_send, col_recv, row_send, row_recv, swap_send, swap_recv,
     cross_send, cross_recv, noise_send, noise_recv, data_send, data_recv,
@@ -109,9 +109,10 @@
     rings = [yi * 2 + ci for yi in (ys[2], ys[1], ys[3], ys[0]) for ci in (1 - core, core)]
     col_peers = [(r, di) for di in (partner * SIDE + z, d) for r in rings][:-1]
     row_peers = [(n, xi * SIDE + zi) for xi in (mate, x) for zi in (zs[2], zs[1], zs[3], zs[0])][:-1]
-    greeted = row_peers + col_peers
-    greeted += [device(opposite, y, z, 0), device(opposite, y, z, 1), device(mate, y, z, 1 - core)]
-    greeted += [device(x, y, around(z + step), 1 - core) for step in (1, -1)]
+    greeted = [sibling]
+    for ci in (0, 1):
+        greeted += [device(partner, y, z, ci), device(mate, y, z, ci), device(x, y, zs[1], ci), device(x, y, zs[3], ci)]
+    greeted += [device(x, ys[1], z, core), device(x, ys[3], z, core)]
     for to in greeted:
         pl.semaphore_signal(barrier, inc=1, device_id=to, device_id_type=MESH)
     pl.semaphore_wait(barrier, len(greeted))
@@ -455,8 +456,23 @@
     colpack[...] = col_pot
     spread_cols()
 
-    def row_step(t, carry):
-        at = tile_at(t)
+    def block_at(b):
+        return pl.ds(pl.multiple_of(b * LANES, LANES), LANES)
+
+    def tiles_of(b):
+        return [pl.ds(pl.multiple_of(b * LANES + q * TILE, TILE), TILE) for q in range(LANES // TILE)]
+
+    def behind(body, compact):
+        def step(b, carry):
+            compact(jnp.maximum(b - 1, 0))
+            for at in tiles_of(b):
+                body(at)
+            return carry
+
+        lax.fori_loop(0, row_blocks, step, 0)
+        compact(row_blocks - 1)
+
+    def row_step(at):
         top = scores[at, lane(0)] + tall(colvec, 0)
         for c in range(1, chunks):
             top = jnp.maximum(top, scores[at, lane(c)] + tall(colvec, c))
@@ -467,71 +483,83 @@
             scores[at, lane(c)] = value
             total = value if total is None else total + value
         part[at, :] = total
-        return carry
-
-    loop(row_step, 0)
-    for b in range(row_blocks):
-        at = pl.ds(b * LANES, LANES)
-        tops = first[at, :].T
+
+    def compact_lse(b):
+        tops = first[block_at(b), :].T
         top = jnp.max(tops, axis=0, keepdims=True)
-        total = jnp.sum(part[at, :].T * jnp.exp2(tops - top), axis=0, keepdims=True)
+        total = jnp.sum(part[block_at(b), :].T * jnp.exp2(tops - top), axis=0, keepdims=True)
         row_buf[0, me_row, pl.ds(b, 1), :] = top + jnp.log(total) * LOG2E
+
+    first[pl.ds(0, LANES), :] = jnp.zeros((LANES, LANES), jnp.float32)
+    behind(row_step, compact_lse)
     exchange(row_buf, row_send, row_recv, 0, me_row, row_peers, started)
     row_lse = combine(row_buf, 0, rsize)
     rowpack[...] = row_lse
-    for b in range(row_blocks):
-        at = pl.ds(b * LANES, LANES)
-        base = jnp.exp2(first[at, :] - spread_lanes(rowpack, b))
-        first[at, :] = base
-        scale[at, :] = base
-
-    def col_step(t, accs):
-        at = tile_at(t)
-        mul = scale[at, :]
-        return tuple(accs[c] + fold(scores[at, lane(c)] * mul, jnp.add) for c in range(chunks))
+
+    def spread_first(b):
+        base = jnp.exp2(first[block_at(b), :] - spread_lanes(rowpack, b))
+        factor_of[block_at(b), :] = base
+        scale[block_at(b), :] = base
+
+    def spread(b):
+        scale[block_at(b), :] = factor_of[block_at(b), :] * spread_lanes(rowpack, b)
+
+    def col_pass(ahead):
+        def step(b, accs):
+            accs = list(accs)
+            for at in tiles_of(b):
+                mul = scale[at, :]
+                for c in range(chunks):
+                    accs[c] = accs[c] + fold(scores[at, lane(c)] * mul, jnp.add)
+            ahead(jnp.minimum(b + 1, row_blocks - 1))
+            return tuple(accs)
+
+        ahead(0)
+        return lax.fori_loop(0, row_blocks, step, zeros)
 
     def sum_step(keep_values):
-        def body(t, carry):
-            at = tile_at(t)
+        def body(at):
             total = None
             for c in range(chunks):
                 value = scores[at, lane(c)] * tall(colvec, c)
                 if keep_values:
                     scores[at, lane(c)] = value
                 total = value if total is None else total + value
-            part[at, :] = total * first[at, :]
-            return carry
+            part[at, :] = total * factor_of[at, :]
 
         return body
 
     for step in range(1, ITERS):
-        sums = loop(col_step, zeros)
+        sums = col_pass(spread_first if step == 1 else spread)
         for c in range(chunks):
             col_buf[step, me_col, pl.ds(c, 1), :] = jnp.sum(sums[c], axis=0, keepdims=True)
         exchange(col_buf, col_send, col_recv, step, me_col, col_peers, started)
         ratio = 1.0 / add_slots(col_buf, step, csize)
         colpack[...] = ratio
         spread_cols()
-        loop(sum_step(step == ITERS - 1), 0)
-        for b in range(row_blocks):
-            at = pl.ds(b * LANES, LANES)
-            row_buf[step, me_row, pl.ds(b, 1), :] = jnp.sum(part[at, :].T, axis=0, keepdims=True)
+
+        def compact(b, step=step):
+            row_buf[step, me_row, pl.ds(b, 1), :] = jnp.sum(part[block_at(b), :].T, axis=0, keepdims=True)
+
+        behind(sum_step(step == ITERS - 1), compact)
         exchange(row_buf, row_send, row_recv, step, me_row, row_peers, started)
         total = add_slots(row_buf, step, rsize)
         rowpack[...] = 1.0 / total
-        for b in range(row_blocks):
-            at = pl.ds(b * LANES, LANES)
-            scale[at, :] = first[at, :] * spread_lanes(rowpack, b)
+    spread(0)
 
     def weigh(r):
-        def body(t, carry):
-            at = pl.ds(pl.multiple_of(r * (rows // 2) + t * TILE, TILE), TILE)
-            mul = scale[at, :]
-            for c in range(chunks):
-                weights[at, lane(c)] = (scores[at, lane(c)] * mul).astype(jnp.bfloat16)
+        blocks = row_blocks // 2
+
+        def body(i, carry):
+            b = r * blocks + i
+            for at in tiles_of(b):
+                mul = scale[at, :]
+                for c in range(chunks):
+                    weights[at, lane(c)] = (scores[at, lane(c)] * mul).astype(jnp.bfloat16)
+            spread(jnp.minimum(b + 1, row_blocks - 1))
             return carry
 
-        lax.fori_loop(0, tiles // 2, body, 0, unroll=2)
+        lax.fori_loop(0, blocks, body, 0)
 
     def swap_copy(i, to):
         return remote(swap.at[0], swap.at[i], swap_send.at[i], swap_recv.at[i], to)
@@ -822,6 +850,7 @@
             pltpu.VMEM((2, SIDE, cols // 2, nsize // SIDE * data_latents.shape[1]), bf16),
             pltpu.VMEM((rows, cols), f32),
             pltpu.VMEM((rows, cols), bf16),
+            pltpu.VMEM((rows, LANES), f32),
             pltpu.VMEM((rows, LANES), f32),
             pltpu.VMEM((rows, LANES), f32),
             pltpu.VMEM((rows, LANES), f32),

time: 127 us -> 128 us (level)
  no operation moved by 1% of the time
where the time goes in v2:
time: 128 us
  Pallas kernels  127 us (99%)
    pallas_call x1, Pallas kernels, shards(): pl.pallas_call(functools.partial(kernel, rsize, csize, piece * dsize), ou...  125 us

profile of v2, /device:TPU:1, one launch (start us, length us, event | category | flops | bytes accessed | tf_op | source)
XLA Modules:
  0.0 128.0 jit_solution(11996703763727441370)
XLA Ops:
  0.6 125.4 %shard_map.49 = (f32[2048,128]{1,0:T(8,128)}, f32[16,128]{1,0:T(8,128)}, f32[8,128]{1,0:T(8,128)}) custom-call(bf16[2048,128]{1,0:T(8,128)(2,1)} %noise_ref.1, bf16[1024,256]{1,0:T(8,128)(2,1)} %data_ref.1), custom_call_target="tpu_custom_call" | custom-call | tf_op jit(solution)/shard_map/pallas_call | solution.py:839
  126.0 2.0 %shard_map.50 = (f32[2048,128]{1,0:T(8,128)}, f32[16,128]{1,0:T(8,128)}, f32[8,128]{1,0:T(8,128)}) custom-call(f32[2048,128]{1,0:T(8,128)} %get-tuple-element.9.targets, f32[16,128]{1,0:T(8,128)} %get-tuple-element.10.rows_pot, f32[8,128]{1,0:T(8,128)} %get-tuple-element.11.cols_pot), custom_call_target="tpu_custom_call" | custom-call | tf_op jit(solution)/shard_map/pallas_call | solution.py:906

commit v3 on v1

--- a/solution.py
+++ b/solution.py
@@ -109,9 +109,10 @@
     rings = [yi * 2 + ci for yi in (ys[2], ys[1], ys[3], ys[0]) for ci in (1 - core, core)]
     col_peers = [(r, di) for di in (partner * SIDE + z, d) for r in rings][:-1]
     row_peers = [(n, xi * SIDE + zi) for xi in (mate, x) for zi in (zs[2], zs[1], zs[3], zs[0])][:-1]
-    greeted = row_peers + col_peers
-    greeted += [device(opposite, y, z, 0), device(opposite, y, z, 1), device(mate, y, z, 1 - core)]
-    greeted += [device(x, y, around(z + step), 1 - core) for step in (1, -1)]
+    greeted = [sibling]
+    for ci in (0, 1):
+        greeted += [device(partner, y, z, ci), device(mate, y, z, ci), device(x, y, zs[1], ci), device(x, y, zs[3], ci)]
+    greeted += [device(x, ys[1], z, core), device(x, ys[3], z, core)]
     for to in greeted:
         pl.semaphore_signal(barrier, inc=1, device_id=to, device_id_type=MESH)
     pl.semaphore_wait(barrier, len(greeted))
@@ -617,7 +618,7 @@
         for t in (0, 1):
             far_copy(b, t).wait_recv()
             out_buf[b, t, half_rows(t), :] = (
-                keep[b - 2, t, half_rows(t), :] + far_buf[b - 2, t].astype(jnp.float32)
+                keep[b - 2, t] + far_buf[b - 2, t].astype(jnp.float32)
             ).astype(jnp.bfloat16)
             added_copy(b, t).start()
 
@@ -641,29 +642,34 @@
 
         lax.fori_loop(0, 2, step, 0)
 
+    def lead(r):
+        t = 1 - r
+        weigh(r)
+        value = product(1, r, around(z + hop(t)))
+        for e in (0, 1):
+            out_buf[2 + e, t, half_rows(r), :] = value[:, lane(e)].astype(jnp.bfloat16)
+        direct_copy(2, t).start()
+
     def give(r):
-        weigh(r)
         value = product(0, r, around(z + 2))
         for e in (0, 1):
             out_buf[e, 2, half_rows(r), :] = value[:, lane(e)].astype(jnp.bfloat16)
         give_copy(0, r).start()
 
-    def near_products(p):
-        def along(t):
-            def part_of(r):
-                value = product(p, r, around(z + hop(t)))
-                for e in (0, 1):
-                    block = value[:, lane(e)]
-                    out_buf[2 * p + e, t, half_rows(r), :] = block.astype(jnp.bfloat16)
-                    if p == 1:
-                        keep[e, t, half_rows(r), :] = block
-
-            halves(part_of)
-            direct_copy(2 * p, t).start()
-            if p == 0:
-                added_copy(0, t).start()
-
-        halves(along)
+    def next_products(t):
+        def part_of(r):
+            value = product(0, r, around(z + hop(t)))
+            for e in (0, 1):
+                out_buf[e, t, half_rows(r), :] = value[:, lane(e)].astype(jnp.bfloat16)
+
+        halves(part_of)
+        direct_copy(0, t).start()
+        added_copy(0, t).start()
+
+    def kept_products(t):
+        value = product(1, t, around(z + hop(t)))
+        for e in (0, 1):
+            keep[e, t] = value[:, lane(e)]
 
     def far_products(r):
         value = product(1, r, around(z + 2))
@@ -678,16 +684,17 @@
 
         halves(part_of)
 
+    halves(lead)
     halves(give)
     for r in (0, 1):
         give_copy(1, r).start()
-    near_products(1)
-    near_products(0)
+    halves(next_products)
     halves(far_products)
     add_given(2)
     for t in (0, 1):
         direct_copy(1, t).start()
         added_copy(1, t).start()
+    halves(kept_products)
     halves(own_products)
     add_near(0)
     for r in (0, 1):
@@ -700,6 +707,16 @@
     mate_out[...] = own_buf[1].astype(jnp.bfloat16)
     mate_copy(core).start()
     potentials()
+    for copy in started:
+        copy.wait_send()
+
+    @pl.when(home)
+    def _():
+        aside.wait_send()
+        for t in (0, 1):
+            for a in (0, 1):
+                own_round(t, a).wait_send()
+
     add_near(2)
 
     def to_partner(r):
@@ -711,6 +728,24 @@
     add_far(3)
     to_partner(1)
 
+    def settle(b, carry):
+        for t in (0, 1):
+            direct_copy(b, t).wait_send()
+            added_copy(b, t).wait_send()
+
+            @pl.when(b < 2)
+            def _():
+                give_copy(jnp.minimum(b, 1), t).wait_send()
+
+            @pl.when(b >= 2)
+            def _():
+                far_copy(jnp.maximum(b, 2), t).wait_send()
+
+        return carry
+
+    lax.fori_loop(0, 3, settle, 0)
+    for r in (0, 1):
+        relay_copy(r).wait_send()
     swap_copy(1, sibling).wait_recv()
     for i in (0, 1):
         remote(swap.at[0], swap.at[2 + i], swap_send.at[2 + i], swap_recv.at[2 + i], sibling).wait_recv()
@@ -742,42 +777,16 @@
     for a in (0, 1):
         result_copy(a).start()
 
-    def settle(b, carry):
-        for t in (0, 1):
-            direct_copy(b, t).wait_send()
-            added_copy(b, t).wait_send()
-
-            @pl.when(b < 2)
-            def _():
-                give_copy(jnp.minimum(b, 1), t).wait_send()
-
-            @pl.when(b >= 2)
-            def _():
-                far_copy(jnp.maximum(b, 2), t).wait_send()
-
-        return carry
-
-    lax.fori_loop(0, SIDE, settle, 0)
+    settle(3, 0)
     for a in (0, 1):
         result_copy(a).wait()
     for r in (0, 1):
-        relay_copy(r).wait_send()
         partner_copy(core, r).wait_send()
     mate_copy(core).wait_send()
 
     @pl.when(jnp.logical_not(home))
     def _():
         stay_copy(core).wait_send()
-
-    for copy in started:
-        copy.wait_send()
-
-    @pl.when(home)
-    def _():
-        aside.wait_send()
-        for t in (0, 1):
-            for a in (0, 1):
-                own_round(t, a).wait_send()
 
 
 def hand_on(targets, rows_pot, cols_pot, targets_out, rows_out, cols_out, stage, row_stage, col_stage, sems):
@@ -856,7 +865,7 @@
             sems((SIDE, 2, 3)),
             sems((6,)),
             sems((6,)),
-            pltpu.VMEM((2, 2, rows, LANES), f32),
+            pltpu.VMEM((2, 2, strip, LANES), f32),
             pltpu.VMEM((2, rows, LANES), f32),
             pltpu.VMEM((2, rows, LANES), bf16),
             sems((2, 2)),

time: 127 us -> 125 us (0.984)
  Pallas kernels: 126 us -> 124 us
    pallas_call x1, Pallas kernels: 124 us -> 122 us  [shards(): pl.pallas_call(functools.partial(kernel, rsize, csize, piece * dsize), ou...]
where the time goes in v3:
time: 125 us
  Pallas kernels  124 us (99%)
    pallas_call x1, Pallas kernels, shards(): pl.pallas_call(functools.partial(kernel, rsize, csize, piece * dsize), ou...  122 us

profile of v3, /device:TPU:1, one launch (start us, length us, event | category | flops | bytes accessed | tf_op | source)
XLA Modules:
  0.0 124.9 jit_solution(11320641758296834154)
XLA Ops:
  0.6 122.2 %shard_map.49 = (f32[2048,128]{1,0:T(8,128)}, f32[16,128]{1,0:T(8,128)}, f32[8,128]{1,0:T(8,128)}) custom-call(bf16[2048,128]{1,0:T(8,128)(2,1)} %noise_ref.1, bf16[1024,256]{1,0:T(8,128)(2,1)} %data_ref.1), custom_call_target="tpu_custom_call" | custom-call | tf_op jit(solution)/shard_map/pallas_call | solution.py:820
  122.8 2.0 %shard_map.50 = (f32[2048,128]{1,0:T(8,128)}, f32[16,128]{1,0:T(8,128)}, f32[8,128]{1,0:T(8,128)}) custom-call(f32[2048,128]{1,0:T(8,128)} %get-tuple-element.9.targets, f32[16,128]{1,0:T(8,128)} %get-tuple-element.10.rows_pot, f32[8,128]{1,0:T(8,128)} %get-tuple-element.11.cols_pot), custom_call_target="tpu_custom_call" | custom-call | tf_op jit(solution)/shard_map/pallas_call | solution.py:886

commit v4 on v3

--- a/solution.py
+++ b/solution.py
@@ -228,6 +228,8 @@
     data_own.start()
     scores[...] = jnp.zeros_like(scores)
     part[...] = jnp.zeros_like(part)
+    shift[...] = jnp.zeros_like(shift)
+    colvec[...] = jnp.zeros_like(colvec)
     data_part[...] = jnp.zeros_like(data_part)
 
     def round_z(xi):
@@ -396,9 +398,17 @@
 
     lax.fori_loop(0, rows // 128, row_shift, 0)
 
+    def exp_sums(m):
+        for e in (0, 1):
+            at = pl.ds(pl.multiple_of(m * 256 + e * LANES, LANES), LANES)
+            top = colvec[0:1, at]
+            total = jnp.sum(jnp.exp2(scores[:, at] + shift[...] - top), axis=0, keepdims=True)
+            col_buf[0, me_col, pl.ds(2 * m + e, 1), :] = top + jnp.log(total) * LOG2E
+
     def final(block, xi):
         def column(i, carry):
             m = block + i
+            exp_sums(block + jnp.maximum(i - 1, 0))
             cut = pl.ds(pl.multiple_of(m * 256, 256), 256)
             value = (scores[:, cut] + chunk_product(xi, m)) * factor
             scores[:, cut] = value
@@ -408,6 +418,7 @@
             return carry
 
         lax.fori_loop(0, 4, column, 0)
+        exp_sums(block + 3)
 
     final(near, opposite)
     add_unit(other_block, jnp.where(opposite == y, 4, jnp.where(opposite == around(y + 2), 0, 2)), opposite)
@@ -439,18 +450,6 @@
 
     zeros = tuple(jnp.zeros((8, LANES), jnp.float32) for _ in range(chunks))
 
-    def exp_step(t, accs):
-        at = tile_at(t)
-        add = shift[at, :]
-        return tuple(
-            accs[c] + fold(jnp.exp2(scores[at, lane(c)] + add - tall(colvec, c)), jnp.add)
-            for c in range(chunks)
-        )
-
-    sums = loop(exp_step, zeros)
-    for c in range(chunks):
-        total = jnp.sum(sums[c], axis=0, keepdims=True)
-        col_buf[0, me_col, pl.ds(c, 1), :] = colvec[0:1, lane(c)] + jnp.log(total) * LOG2E
     exchange(col_buf, col_send, col_recv, 0, me_col, col_peers, started)
     col_pot = -log_cols - combine(col_buf, 0, csize)
     colpack[...] = col_pot
@@ -693,16 +692,25 @@
     add_given(2)
     for t in (0, 1):
         direct_copy(1, t).start()
-        added_copy(1, t).start()
     halves(kept_products)
     halves(own_products)
     add_near(0)
     for r in (0, 1):
         relay_copy(r).start()
     add_far(2)
+    for t in (0, 1):
+        added_copy(1, t).start()
     add_given(3)
     for t in (0, 1):
         direct_copy(3, t).start()
+    add_near(2)
+
+    def to_partner(r):
+        relay_copy(r).wait_recv()
+        own_buf[2, half_rows(r), :] = own_buf[2, half_rows(r), :] + relay_in[half_rows(r), :]
+        partner_copy(core, r).start()
+
+    to_partner(0)
     add_near(1)
     mate_out[...] = own_buf[1].astype(jnp.bfloat16)
     mate_copy(core).start()
@@ -717,14 +725,6 @@
             for a in (0, 1):
                 own_round(t, a).wait_send()
 
-    add_near(2)
-
-    def to_partner(r):
-        relay_copy(r).wait_recv()
-        own_buf[2, half_rows(r), :] = own_buf[2, half_rows(r), :] + relay_in[half_rows(r), :]
-        partner_copy(core, r).start()
-
-    to_partner(0)
     add_far(3)
     to_partner(1)
 

time: 125 us -> 126 us (level)
  no operation moved by 1% of the time
where the time goes in v4:
time: 126 us
  Pallas kernels  125 us (99%)
    pallas_call x1, Pallas kernels, shards(): pl.pallas_call(functools.partial(kernel, rsize, csize, piece * dsize), ou...  123 us

profile of v4, /device:TPU:1, one launch (start us, length us, event | category | flops | bytes accessed | tf_op | source)
XLA Modules:
  0.0 125.6 jit_solution(14758797402751176046)
XLA Ops:
  0.6 122.8 %shard_map.49 = (f32[2048,128]{1,0:T(8,128)}, f32[16,128]{1,0:T(8,128)}, f32[8,128]{1,0:T(8,128)}) custom-call(bf16[2048,128]{1,0:T(8,128)(2,1)} %noise_ref.1, bf16[1024,256]{1,0:T(8,128)(2,1)} %data_ref.1), custom_call_target="tpu_custom_call" | custom-call | tf_op jit(solution)/shard_map/pallas_call | solution.py:820
  123.4 2.0 %shard_map.50 = (f32[2048,128]{1,0:T(8,128)}, f32[16,128]{1,0:T(8,128)}, f32[8,128]{1,0:T(8,128)}) custom-call(f32[2048,128]{1,0:T(8,128)} %get-tuple-element.9.targets, f32[16,128]{1,0:T(8,128)} %get-tuple-element.10.rows_pot, f32[8,128]{1,0:T(8,128)} %get-tuple-element.11.cols_pot), custom_call_target="tpu_custom_call" | custom-call | tf_op jit(solution)/shard_map/pallas_call | solution.py:886

commit v5 on v3

--- a/solution.py
+++ b/solution.py
@@ -693,16 +693,25 @@
     add_given(2)
     for t in (0, 1):
         direct_copy(1, t).start()
-        added_copy(1, t).start()
     halves(kept_products)
     halves(own_products)
     add_near(0)
     for r in (0, 1):
         relay_copy(r).start()
     add_far(2)
+    for t in (0, 1):
+        added_copy(1, t).start()
     add_given(3)
     for t in (0, 1):
         direct_copy(3, t).start()
+    add_near(2)
+
+    def to_partner(r):
+        relay_copy(r).wait_recv()
+        own_buf[2, half_rows(r), :] = own_buf[2, half_rows(r), :] + relay_in[half_rows(r), :]
+        partner_copy(core, r).start()
+
+    to_partner(0)
     add_near(1)
     mate_out[...] = own_buf[1].astype(jnp.bfloat16)
     mate_copy(core).start()
@@ -717,14 +726,6 @@
             for a in (0, 1):
                 own_round(t, a).wait_send()
 
-    add_near(2)
-
-    def to_partner(r):
-        relay_copy(r).wait_recv()
-        own_buf[2, half_rows(r), :] = own_buf[2, half_rows(r), :] + relay_in[half_rows(r), :]
-        partner_copy(core, r).start()
-
-    to_partner(0)
     add_far(3)
     to_partner(1)
 

time: 125 us -> 124 us (level)
    pallas_call x1, Pallas kernels: 122 us -> 121 us  [shards(): pl.pallas_call(functools.partial(kernel, rsize, csize, piece * dsize), ou...]
where the time goes in v5:
time: 124 us; the launch traced here: 123 us
  Pallas kernels  123 us (99%)
    pallas_call x1, Pallas kernels, shards(): pl.pallas_call(functools.partial(kernel, rsize, csize, piece * dsize), ou...  121 us

profile of v5, /device:TPU:1, one launch (start us, length us, event | category | flops | bytes accessed | tf_op | source)
XLA Modules:
  0.0 123.5 jit_solution(10743344168000415365)
XLA Ops:
  0.6 120.8 %shard_map.49 = (f32[2048,128]{1,0:T(8,128)}, f32[16,128]{1,0:T(8,128)}, f32[8,128]{1,0:T(8,128)}) custom-call(bf16[2048,128]{1,0:T(8,128)(2,1)} %noise_ref.1, bf16[1024,256]{1,0:T(8,128)(2,1)} %data_ref.1), custom_call_target="tpu_custom_call" | custom-call | tf_op jit(solution)/shard_map/pallas_call | solution.py:821
  121.4 2.0 %shard_map.50 = (f32[2048,128]{1,0:T(8,128)}, f32[16,128]{1,0:T(8,128)}, f32[8,128]{1,0:T(8,128)}) custom-call(f32[2048,128]{1,0:T(8,128)} %get-tuple-element.9.targets, f32[16,128]{1,0:T(8,128)} %get-tuple-element.10.rows_pot, f32[8,128]{1,0:T(8,128)} %get-tuple-element.11.cols_pot), custom_call_target="tpu_custom_call" | custom-call | tf_op jit(solution)/shard_map/pallas_call | solution.py:887

commit v6 on v5

--- a/solution.py
+++ b/solution.py
@@ -14,6 +14,8 @@
 MESH = pl.DeviceIdType.MESH
 LANES = 128
 TILE = 32
+SHORT = 16
+TALL = 64
 SIDE = 4
 PARTS = 4
 
@@ -420,7 +422,7 @@
 
     def fold(block, op):
         out = block[0:8]
-        for r in range(1, TILE // 8):
+        for r in range(1, block.shape[0] // 8):
             out = op(out, block[8 * r:8 * r + 8])
         return out
 
@@ -428,8 +430,8 @@
         for c in range(chunks):
             colvec[:, lane(c)] = jnp.broadcast_to(colpack[pl.ds(c, 1), :], (8, LANES))
 
-    def tall(ref, c):
-        return jnp.concatenate([ref[:, lane(c)]] * (TILE // 8), axis=0)
+    def tall(ref, c, size=TILE):
+        return jnp.concatenate([ref[:, lane(c)]] * (size // 8), axis=0)
 
     def tile_at(t):
         return pl.ds(pl.multiple_of(t * TILE, TILE), TILE)
@@ -440,14 +442,14 @@
     zeros = tuple(jnp.zeros((8, LANES), jnp.float32) for _ in range(chunks))
 
     def exp_step(t, accs):
-        at = tile_at(t)
+        at = pl.ds(pl.multiple_of(t * TALL, TALL), TALL)
         add = shift[at, :]
         return tuple(
-            accs[c] + fold(jnp.exp2(scores[at, lane(c)] + add - tall(colvec, c)), jnp.add)
+            accs[c] + fold(jnp.exp2(scores[at, lane(c)] + add - tall(colvec, c, TALL)), jnp.add)
             for c in range(chunks)
         )
 
-    sums = loop(exp_step, zeros)
+    sums = lax.fori_loop(0, rows // TALL, exp_step, zeros)
     for c in range(chunks):
         total = jnp.sum(sums[c], axis=0, keepdims=True)
         col_buf[0, me_col, pl.ds(c, 1), :] = colvec[0:1, lane(c)] + jnp.log(total) * LOG2E
@@ -457,20 +459,23 @@
     spread_cols()
 
     def row_step(t, carry):
-        at = tile_at(t)
-        top = scores[at, lane(0)] + tall(colvec, 0)
+        at = pl.ds(pl.multiple_of(t * SHORT, SHORT), SHORT)
+        values = [
+            scores[at, lane(c)] + jnp.concatenate([colvec[:, lane(c)]] * (SHORT // 8), axis=0) for c in range(chunks)
+        ]
+        top = values[0]
         for c in range(1, chunks):
-            top = jnp.maximum(top, scores[at, lane(c)] + tall(colvec, c))
+            top = jnp.maximum(top, values[c])
         first[at, :] = top
         total = None
         for c in range(chunks):
-            value = jnp.exp2(scores[at, lane(c)] + tall(colvec, c) - top)
+            value = jnp.exp2(values[c] - top)
             scores[at, lane(c)] = value
             total = value if total is None else total + value
         part[at, :] = total
         return carry
 
-    loop(row_step, 0)
+    lax.fori_loop(0, rows // SHORT, row_step, 0, unroll=2)
     for b in range(row_blocks):
         at = pl.ds(b * LANES, LANES)
         tops = first[at, :].T
@@ -493,10 +498,10 @@
 
     def sum_step(keep_values):
         def body(t, carry):
-            at = tile_at(t)
+            at = pl.ds(pl.multiple_of(t * TALL, TALL), TALL)
             total = None
             for c in range(chunks):
-                value = scores[at, lane(c)] * tall(colvec, c)
+                value = scores[at, lane(c)] * tall(colvec, c, TALL)
                 if keep_values:
                     scores[at, lane(c)] = value
                 total = value if total is None else total + value
@@ -513,7 +518,7 @@
         ratio = 1.0 / add_slots(col_buf, step, csize)
         colpack[...] = ratio
         spread_cols()
-        loop(sum_step(step == ITERS - 1), 0)
+        lax.fori_loop(0, rows // TALL, sum_step(step == ITERS - 1), 0)
         for b in range(row_blocks):
             at = pl.ds(b * LANES, LANES)
             row_buf[step, me_row, pl.ds(b, 1), :] = jnp.sum(part[at, :].T, axis=0, keepdims=True)

time: 124 us -> 125 us (level)
  no operation moved by 1% of the time
where the time goes in v6:
time: 125 us; the launch traced here: 124 us
  Pallas kernels  124 us (99%)
    pallas_call x1, Pallas kernels, shards(): pl.pallas_call(functools.partial(kernel, rsize, csize, piece * dsize), ou...  122 us

profile of v6, /device:TPU:1, one launch (start us, length us, event | category | flops | bytes accessed | tf_op | source)
XLA Modules:
  0.0 124.2 jit_solution(14080516728093279739)
XLA Ops:
  0.6 121.6 %shard_map.49 = (f32[2048,128]{1,0:T(8,128)}, f32[16,128]{1,0:T(8,128)}, f32[8,128]{1,0:T(8,128)}) custom-call(bf16[2048,128]{1,0:T(8,128)(2,1)} %noise_ref.1, bf16[1024,256]{1,0:T(8,128)(2,1)} %data_ref.1), custom_call_target="tpu_custom_call" | custom-call | tf_op jit(solution)/shard_map/pallas_call | solution.py:826
  122.2 2.0 %shard_map.50 = (f32[2048,128]{1,0:T(8,128)}, f32[16,128]{1,0:T(8,128)}, f32[8,128]{1,0:T(8,128)}) custom-call(f32[2048,128]{1,0:T(8,128)} %get-tuple-element.9.targets, f32[16,128]{1,0:T(8,128)} %get-tuple-element.10.rows_pot, f32[8,128]{1,0:T(8,128)} %get-tuple-element.11.cols_pot), custom_call_target="tpu_custom_call" | custom-call | tf_op jit(solution)/shard_map/pallas_call | solution.py:892

commit v7 on v6

--- a/solution.py
+++ b/solution.py
@@ -230,7 +230,6 @@
     data_own.start()
     scores[...] = jnp.zeros_like(scores)
     part[...] = jnp.zeros_like(part)
-    data_part[...] = jnp.zeros_like(data_part)
 
     def round_z(xi):
         for t in (0, 1):
@@ -296,12 +295,7 @@
         return value * value
 
     def chunk_product(xi, m):
-        cut = pl.ds(pl.multiple_of(m * 256, 256), 256)
         here = pl.ds(pl.multiple_of(lax.rem(m, 4) * 256, 256), 256)
-        total = data_part[cut, :]
-        for i in range(SIDE):
-            total = total + squares(data_all[m // 4, xi, here, lane(i)])
-        data_part[cut, :] = total
         return lax.dot_general(
             noise_all[xi], data_all[m // 4, xi, here, :], (((1,), (1,)), ((), ())),
             preferred_element_type=jnp.float32,
@@ -709,6 +703,18 @@
     add_given(3)
     for t in (0, 1):
         direct_copy(3, t).start()
+    def data_norms(r, carry):
+        per = full_cols // 64
+        here = pl.ds(pl.multiple_of(lax.rem(r, per) * 64, 64), 64)
+        total = None
+        for xi in range(SIDE):
+            for i in range(SIDE):
+                value = squares(data_all[r // per, xi, here, lane(i)])
+                total = value if total is None else total + value
+        data_part[pl.ds(pl.multiple_of(r * 64, 64), 64), :] = total
+        return carry
+
+    lax.fori_loop(0, cols // 64, data_norms, 0)
     add_near(2)
 
     def to_partner(r):

time: 125 us -> 124 us (level)
  no operation moved by 1% of the time
where the time goes in v7:
time: 124 us
  Pallas kernels  123 us (99%)
    pallas_call x1, Pallas kernels, shards(): pl.pallas_call(functools.partial(kernel, rsize, csize, piece * dsize), ou...  121 us

profile of v7, /device:TPU:1, one launch (start us, length us, event | category | flops | bytes accessed | tf_op | source)
XLA Modules:
  0.0 124.1 jit_solution(6057385738107827000)
XLA Ops:
  0.6 121.4 %shard_map.49 = (f32[2048,128]{1,0:T(8,128)}, f32[16,128]{1,0:T(8,128)}, f32[8,128]{1,0:T(8,128)}) custom-call(bf16[2048,128]{1,0:T(8,128)(2,1)} %noise_ref.1, bf16[1024,256]{1,0:T(8,128)(2,1)} %data_ref.1), custom_call_target="tpu_custom_call" | custom-call | tf_op jit(solution)/shard_map/pallas_call | solution.py:832
  122.1 2.0 %shard_map.50 = (f32[2048,128]{1,0:T(8,128)}, f32[16,128]{1,0:T(8,128)}, f32[8,128]{1,0:T(8,128)}) custom-call(f32[2048,128]{1,0:T(8,128)} %get-tuple-element.9.targets, f32[16,128]{1,0:T(8,128)} %get-tuple-element.10.rows_pot, f32[8,128]{1,0:T(8,128)} %get-tuple-element.11.cols_pot), custom_call_target="tpu_custom_call" | custom-call | tf_op jit(solution)/shard_map/pallas_call | solution.py:898

commit v8 on v7

--- a/solution.py
+++ b/solution.py
@@ -294,10 +294,11 @@
         value = block.astype(jnp.float32)
         return value * value
 
-    def chunk_product(xi, m):
-        here = pl.ds(pl.multiple_of(lax.rem(m, 4) * 256, 256), 256)
+    def chunk_product(xi, m, size=256):
+        per = full_cols // size
+        here = pl.ds(pl.multiple_of(lax.rem(m, per) * size, size), size)
         return lax.dot_general(
-            noise_all[xi], data_all[m // 4, xi, here, :], (((1,), (1,)), ((), ())),
+            noise_all[xi], data_all[m // per, xi, here, :], (((1,), (1,)), ((), ())),
             preferred_element_type=jnp.float32,
         )
 
@@ -314,13 +315,14 @@
 
     near, other_block = side * 4, 4 - side * 4
 
-    def unit(block, xs, fresh, count=4):
+    def unit(block, xs, fresh, count=2):
         def column(i, carry):
             m = block + i
-            cut = pl.ds(pl.multiple_of(m * 256, 256), 256)
+            cut = pl.ds(pl.multiple_of(m * 512, 512), 512)
             value = None if fresh else scores[:, cut]
             for xi in xs:
-                value = chunk_product(xi, m) if value is None else value + chunk_product(xi, m)
+                product = chunk_product(xi, m, 512)
+                value = product if value is None else value + product
             scores[:, cut] = value
             return carry
 
@@ -344,13 +346,13 @@
     def _():
         cross_wait(x)
 
-    unit(near, (x,), True)
+    unit(near // 2, (x,), True)
     share_far(partner)
     norms(x)
     for t in (0, 1):
         noise_wait(mate, t, False)
     far_wait(mate)
-    unit(near, (mate,), False)
+    unit(near // 2, (mate,), False)
     norms(mate)
 
     def beside(t, h, c):
@@ -359,7 +361,7 @@
     for t in (0, 1):
         partner_wait(t, 0)
         begin(beside(t, 0, core))
-    unit(near, (partner,), False)
+    unit(near // 2, (partner,), False)
     norms(partner)
     data_wait(1, 4, along_y(0, 1 - core), 0, full_cols)
     for t in (0, 1):
@@ -367,7 +369,7 @@
 
     def ahead(i, carry):
         xi = around(y + i + i // 2)
-        add_unit(other_block, jnp.where(xi == opposite, 0, jnp.where(i == 0, 4, 2)), xi)
+        add_unit(other_block // 2, jnp.where(xi == opposite, 0, jnp.where(i == 0, 2, 1)), xi)
         return carry
 
     lax.fori_loop(0, 3, ahead, 0)
@@ -406,10 +408,10 @@
         lax.fori_loop(0, 4, column, 0)
 
     final(near, opposite)
-    add_unit(other_block, jnp.where(opposite == y, 4, jnp.where(opposite == around(y + 2), 0, 2)), opposite)
+    add_unit(other_block // 2, jnp.where(opposite == y, 2, jnp.where(opposite == around(y + 2), 0, 1)), opposite)
     for t in (0, 1):
         beside(t, 1, 1 - core).wait_recv()
-    unit(other_block + 2, (around(y + 1), around(y - 1)), False, 2)
+    unit(other_block // 2 + 1, (around(y + 1), around(y - 1)), False, 1)
     for t in (0, 1):
         data_wait(1, 7 + t, along_y(2, 1 - core), t * half_cols, half_cols)
     final(other_block, around(y + 2))

time: 124 us -> 123 us (level)
    pallas_call x1, Pallas kernels: 121 us -> 120 us  [shards(): pl.pallas_call(functools.partial(kernel, rsize, csize, piece * dsize), ou...]
where the time goes in v8:
time: 123 us
  Pallas kernels  122 us (99%)
    pallas_call x1, Pallas kernels, shards(): pl.pallas_call(functools.partial(kernel, rsize, csize, piece * dsize), ou...  120 us

profile of v8, /device:TPU:1, one launch (start us, length us, event | category | flops | bytes accessed | tf_op | source)
XLA Modules:
  0.0 122.9 jit_solution(4652090510911988999)
XLA Ops:
  0.6 120.1 %shard_map.49 = (f32[2048,128]{1,0:T(8,128)}, f32[16,128]{1,0:T(8,128)}, f32[8,128]{1,0:T(8,128)}) custom-call(bf16[2048,128]{1,0:T(8,128)(2,1)} %noise_ref.1, bf16[1024,256]{1,0:T(8,128)(2,1)} %data_ref.1), custom_call_target="tpu_custom_call" | custom-call | tf_op jit(solution)/shard_map/pallas_call | solution.py:834
  120.7 2.0 %shard_map.50 = (f32[2048,128]{1,0:T(8,128)}, f32[16,128]{1,0:T(8,128)}, f32[8,128]{1,0:T(8,128)}) custom-call(f32[2048,128]{1,0:T(8,128)} %get-tuple-element.9.targets, f32[16,128]{1,0:T(8,128)} %get-tuple-element.10.rows_pot, f32[8,128]{1,0:T(8,128)} %get-tuple-element.11.cols_pot), custom_call_target="tpu_custom_call" | custom-call | tf_op jit(solution)/shard_map/pallas_call | solution.py:900

commit v9 on v8

--- a/solution.py
+++ b/solution.py
@@ -397,24 +397,24 @@
     def final(block, xi):
         def column(i, carry):
             m = block + i
-            cut = pl.ds(pl.multiple_of(m * 256, 256), 256)
-            value = (scores[:, cut] + chunk_product(xi, m)) * factor
+            cut = pl.ds(pl.multiple_of(m * 512, 512), 512)
+            value = (scores[:, cut] + chunk_product(xi, m, 512)) * factor
             scores[:, cut] = value
-            for e in (0, 1):
-                top = jnp.max(value[:, LANES * e:LANES * (e + 1)] + shift[...], axis=0, keepdims=True)
-                colvec[:, pl.ds(pl.multiple_of(m * 256 + e * LANES, LANES), LANES)] = jnp.broadcast_to(top, (8, LANES))
+            for e in range(SIDE):
+                top = jnp.max(value[:, lane(e)] + shift[...], axis=0, keepdims=True)
+                colvec[:, pl.ds(pl.multiple_of(m * 512 + e * LANES, LANES), LANES)] = jnp.broadcast_to(top, (8, LANES))
             return carry
 
-        lax.fori_loop(0, 4, column, 0)
-
-    final(near, opposite)
+        lax.fori_loop(0, 2, column, 0)
+
+    final(near // 2, opposite)
     add_unit(other_block // 2, jnp.where(opposite == y, 2, jnp.where(opposite == around(y + 2), 0, 1)), opposite)
     for t in (0, 1):
         beside(t, 1, 1 - core).wait_recv()
     unit(other_block // 2 + 1, (around(y + 1), around(y - 1)), False, 1)
     for t in (0, 1):
         data_wait(1, 7 + t, along_y(2, 1 - core), t * half_cols, half_cols)
-    final(other_block, around(y + 2))
+    final(other_block // 2, around(y + 2))
 
     def fold(block, op):
         out = block[0:8]

time: 123 us -> 122 us (level)
  no operation moved by 1% of the time
where the time goes in v9:
time: 122 us
  Pallas kernels  121 us (99%)
    pallas_call x1, Pallas kernels, shards(): pl.pallas_call(functools.partial(kernel, rsize, csize, piece * dsize), ou...  119 us

profile of v9, /device:TPU:1, one launch (start us, length us, event | category | flops | bytes accessed | tf_op | source)
XLA Modules:
  0.0 122.1 jit_solution(5328558654646670544)
XLA Ops:
  0.6 119.2 %shard_map.49 = (f32[2048,128]{1,0:T(8,128)}, f32[16,128]{1,0:T(8,128)}, f32[8,128]{1,0:T(8,128)}) custom-call(bf16[2048,128]{1,0:T(8,128)(2,1)} %noise_ref.1, bf16[1024,256]{1,0:T(8,128)(2,1)} %data_ref.1), custom_call_target="tpu_custom_call" | custom-call | tf_op jit(solution)/shard_map/pallas_call | solution.py:834
  119.9 2.0 %shard_map.50 = (f32[2048,128]{1,0:T(8,128)}, f32[16,128]{1,0:T(8,128)}, f32[8,128]{1,0:T(8,128)}) custom-call(f32[2048,128]{1,0:T(8,128)} %get-tuple-element.9.targets, f32[16,128]{1,0:T(8,128)} %get-tuple-element.10.rows_pot, f32[8,128]{1,0:T(8,128)} %get-tuple-element.11.cols_pot), custom_call_target="tpu_custom_call" | custom-call | tf_op jit(solution)/shard_map/pallas_call | solution.py:900
